TPU v7x, 256 devices: a whole 4x4x8 slice. The times are simulated.
256 devices in a mesh: seq: 64 (over y_lo, x, z), dp: 4 (over y_hi, core).
Axes of the slice: x: 4, y: 4 (y_hi: 2, y_lo: 2; y = y_hi * 2 + y_lo), z: 8, core: 2. Of those that a mesh axis runs over, the one named last changes fastest.
Arguments:
- signal: float32 [4, 65536, 384], P('dp', 'seq'), may hold values from -6 to 6
- gate_values: float32 [4, 65536, 384], P('dp', 'seq'), may hold values from -6 to 6
- cotangent: float32 [4, 65536, 384], P('dp', 'seq'), may hold values from -6 to 6
- kernel: float32 [128, 512, 384], P(None, 'seq'), may hold values from -6 to 6
- first_factor: float32 [128, 128], replicated, may hold values from -0.5 to 0.5
- second_factor: float32 [512, 512], replicated, may hold values from -0.25 to 0.25
Outputs:
- grad_signal: float32 [4, 65536, 384], P('dp', 'seq')
- grad_gates: float32 [4, 65536, 384], P('dp', 'seq')
- grad_kernel: float32 [128, 512, 384], P('dp', 'seq')
- grad_first: float32 [128, 128], replicated
- grad_second: float32 [512, 512], replicated
All inputs are finite; a program needn't handle non-finite values.
Results may differ from a plain program's by a relative error of at most 0.000071.
Values sent between devices are 32-bit elements; how exact they have to be, the bound alone decides.
No kernel may reach another device: no remote copies, remote signals or barrier semaphores. Data moves between devices by JAX's collectives and lax.ppermute only.
A program may use at most 128 MiB of HBM per device.

v0:
```python
import math
import jax
import jax.numpy as jnp
from jax import lax
from jax.sharding import PartitionSpec as P


def along_second(data, factor):
    return jnp.einsum("bijc,kj->bikc", data, factor, precision=lax.Precision.HIGHEST)


def along_second_t(data, factor):
    return jnp.einsum("bikc,kj->bijc", data, factor, precision=lax.Precision.HIGHEST)


def along_first(factor, data):
    return jnp.einsum("mi,bikc->bmkc", factor, data, precision=lax.Precision.HIGHEST)


def along_first_t(factor, data):
    return jnp.einsum("mi,bmkc->bikc", factor, data, precision=lax.Precision.HIGHEST)


def outer_first(left, right):
    return jnp.einsum("bmkc,bikc->mi", left, right, precision=lax.Precision.HIGHEST)


def outer_second(left, right):
    return jnp.einsum("bikc,bijc->kj", left, right, precision=lax.Precision.HIGHEST)


def body(signal, gate_values, cotangent, kernel, first_factor, second_factor):
    batch = signal.shape[0]
    blocks = first_factor.shape[0]
    block = second_factor.shape[0]
    channels = signal.shape[2]
    local_rows = signal.shape[1] // block
    shape_rows = (batch, local_rows, block, channels)
    source = signal.reshape(shape_rows)
    gating = gate_values.reshape(shape_rows)
    upstream = cotangent.reshape(shape_rows)
    whole = lax.all_to_all(source, "seq", split_axis=3, concat_axis=1, tiled=True)
    kernel_cols = lax.all_to_all(kernel, "seq", split_axis=2, concat_axis=1, tiled=True)
    section_one = along_second(whole, second_factor)
    spectrum = along_first(first_factor, section_one)
    weighted = kernel_cols[None] * spectrum
    back_one = along_first_t(first_factor, weighted)
    full_mixed = along_second_t(back_one, second_factor)
    mixed = lax.all_to_all(full_mixed, "seq", split_axis=1, concat_axis=3, tiled=True)
    grad_mixed = upstream * gating
    grad_gate = upstream * mixed
    grad_whole = lax.all_to_all(grad_mixed, "seq", split_axis=3, concat_axis=1, tiled=True)
    grad_back = along_second(grad_whole, second_factor)
    second_grad = outer_second(back_one, grad_whole)
    grad_weighted = along_first(first_factor, grad_back)
    first_grad = outer_first(weighted, grad_back)
    kernel_cols_grad = jnp.sum(grad_weighted * spectrum, axis=0)
    grad_spectrum = grad_weighted * kernel_cols[None]
    grad_section = along_first_t(first_factor, grad_spectrum)
    first_grad = first_grad + outer_first(grad_spectrum, section_one)
    grad_full = along_second_t(grad_section, second_factor)
    second_grad = second_grad + outer_second(grad_section, whole)
    grad_source = lax.all_to_all(grad_full, "seq", split_axis=1, concat_axis=3, tiled=True)
    kernel_term = lax.all_to_all(kernel_cols_grad, "seq", split_axis=1, concat_axis=2, tiled=True)
    grad_kernel = lax.psum_scatter(kernel_term, "dp", scatter_dimension=0, tiled=True)
    first_total, second_total = lax.psum((first_grad, second_grad), ("seq", "dp"))
    sequences = batch * lax.axis_size("dp")
    first_scale = 1.0 / math.sqrt(sequences * block * channels)
    second_scale = 1.0 / math.sqrt(sequences * blocks * channels)
    return (
        grad_source.reshape(signal.shape),
        grad_gate.reshape(signal.shape),
        grad_kernel,
        first_total * first_scale,
        second_total * second_scale,
    )


def solution(mesh):
    in_specs = (
        P("dp", "seq", None),
        P("dp", "seq", None),
        P("dp", "seq", None),
        P(None, "seq", None),
        P(),
        P(),
    )
    out_specs = (P("dp", "seq", None), P("dp", "seq", None), P("dp", "seq", None), P(), P())
    return jax.shard_map(body, mesh=mesh, in_specs=in_specs, out_specs=out_specs, check_vma=False)
```

profile of v0, /device:TPU:6, one launch (start us, length us, event | category | flops | bytes accessed | tf_op | source)
XLA Modules:
  0.0 535.5 jit_solution(2666855981043520354)
XLA Ops:
  8.0 3.8 copy.114
  11.8 13.0 %all-to-all-start.3 = ((f32[1,2,512,384]{2,1,0,3:T(2,128)}), f32[1,2,512,384]{2,1,0,3:T(2,128)S(1)}, u32[]{:S(2)}, u32[]{:S(2)}) async-start(f32[1,2,512,384]{2,1,0,3:T(2,128)} %copy.114), calls=%async_computation.3 | async-start | bytes 3145728 | tf_op jit(solution)/shard_map/all_to_all | solution.py:42
  24.8 3.2 mul.41
  28.0 3.7 copy.113
  31.7 32.9 %all-to-all-done.3 = f32[1,2,512,384]{2,1,0,3:T(2,128)S(1)} async-done(((f32[1,2,512,384]{2,1,0,3:T(2,128)}), f32[1,2,512,384]{2,1,0,3:T(2,128)S(1)}, u32[]{:S(2)}, u32[]{:S(2)}) %all-to-all-start.3) | async-done | bytes 1572896 | tf_op jit(solution)/shard_map/all_to_all | solution.py:42
  64.6 6.6 %all-to-all-start = ((f32[1,2,512,384]{2,1,0,3:T(2,128)}), f32[1,2,512,384]{2,1,0,3:T(2,128)}, u32[]{:S(2)}, u32[]{:S(2)}) async-start(f32[1,2,512,384]{2,1,0,3:T(2,128)} %copy.113), calls=%async_computation | async-start | bytes 3145728 | tf_op jit(solution)/shard_map/all_to_all | solution.py:52
  71.2 3.1 copy.87
  74.3 35.7 %all-to-all-done = f32[1,2,512,384]{2,1,0,3:T(2,128)} async-done(((f32[1,2,512,384]{2,1,0,3:T(2,128)}), f32[1,2,512,384]{2,1,0,3:T(2,128)}, u32[]{:S(2)}, u32[]{:S(2)}) %all-to-all-start) | async-done | bytes 1572896 | tf_op jit(solution)/shard_map/all_to_all | solution.py:52
  110.0 6.3 %all-to-all-start.1 = ((f32[128,8,384]{0,1,2:T(8,128)}), f32[128,8,384]{0,1,2:T(8,128)S(1)}, u32[]{:S(2)}, u32[]{:S(2)}) async-start(f32[128,8,384]{0,1,2:T(8,128)} %copy.87), calls=%async_computation.1 | async-start | bytes 3145728 | tf_op jit(solution)/shard_map/all_to_all | solution.py:43
  116.3 3.1 copy.93
  119.4 3.1 reshape.99
  122.5 3.1 copy.85
  125.6 3.3 reshape.93
  129.0 4.2 fusion.44
  133.2 1.5 fusion.10
  135.2 2.7 fusion.47
  137.9 2.6 fusion.14
  141.6 2.2 copy.98
  143.9 10.8 %all-to-all-done.1 = f32[128,8,384]{0,1,2:T(8,128)S(1)} async-done(((f32[128,8,384]{0,1,2:T(8,128)}), f32[128,8,384]{0,1,2:T(8,128)S(1)}, u32[]{:S(2)}, u32[]{:S(2)}) %all-to-all-start.1) | async-done | bytes 1572896 | tf_op jit(solution)/shard_map/all_to_all | solution.py:43
  154.6 6.9 %all-to-all-start.5 = ((f32[128,512,6]{0,2,1:T(8,128)}), f32[128,512,6]{0,2,1:T(8,128)}, u32[]{:S(2)}, u32[]{:S(2)}) async-start(f32[128,512,6]{0,2,1:T(8,128)} %copy.98), calls=%async_computation.5 | async-start | bytes 4194304 | tf_op jit(solution)/shard_map/all_to_all | solution.py:64
  161.5 2.8 fusion.53
  165.5 2.7 fusion.19
  168.2 2.9 copy.95
  171.1 38.3 %all-to-all-done.5 = f32[128,512,6]{0,2,1:T(8,128)} async-done(((f32[128,512,6]{0,2,1:T(8,128)}), f32[128,512,6]{0,2,1:T(8,128)}, u32[]{:S(2)}, u32[]{:S(2)}) %all-to-all-start.5) | async-done | bytes 1572896 | tf_op jit(solution)/shard_map/all_to_all | solution.py:64
  209.4 6.8 %all-to-all-start.4 = ((f32[1,128,512,6]{2,0,3,1:T(1,128)}), f32[1,128,512,6]{2,0,3,1:T(1,128)}, u32[]{:S(2)}, u32[]{:S(2)}) async-start(f32[1,128,512,6]{2,0,3,1:T(1,128)} %copy.95), calls=%async_computation.4 | async-start | bytes 3145728 | tf_op jit(solution)/shard_map/all_to_all | solution.py:49
  216.6 4.7 fusion.25
  221.4 2.7 fusion.34
  224.1 1.4 fusion.50
  225.6 3.4 fusion.40
  229.0 3.7 fusion.31
  232.9 1.9 copy.100
  234.9 1.8 copy.101
  236.7 1.4 copy-done.12
  238.1 2.7 fusion.22
  240.7 2.8 copy.90
  243.5 9.3 %all-to-all-done.4 = f32[1,128,512,6]{2,0,3,1:T(1,128)} async-done(((f32[1,128,512,6]{2,0,3,1:T(1,128)}), f32[1,128,512,6]{2,0,3,1:T(1,128)}, u32[]{:S(2)}, u32[]{:S(2)}) %all-to-all-start.4) | async-done | bytes 1572896 | tf_op jit(solution)/shard_map/all_to_all | solution.py:49
  252.7 6.8 %all-to-all-start.2 = ((f32[1,128,512,6]{2,0,3,1:T(1,128)}), f32[1,128,512,6]{2,0,3,1:T(1,128)S(1)}, u32[]{:S(2)}, u32[]{:S(2)}) async-start(f32[1,128,512,6]{2,0,3,1:T(1,128)} %copy.90), calls=%async_computation.2 | async-start | bytes 3145728 | tf_op jit(solution)/shard_map/all_to_all | solution.py:63
  259.6 3.0 copy.97
  262.6 242.0 %all-reduce.3.cloned.1.call-done = (f32[128,128]{1,0:T(8,128)}, f32[512,512]{1,0:T(8,128)}) async-done(((f32[128,128]{1,0:T(8,128)}, f32[512,512]{1,0:T(8,128)}), (f32[128,128]{1,0:T(8,128)}, f32[512,512]{1,0:T(8,128)})) %all-reduce.3.cloned.1.call-update) | async-done | bytes 1114128 | tf_op jit(solution)/shard_map/psum | solution.py:66
  504.6 1.5 broadcast_multiply_fusion.1
  506.1 2.3 broadcast_multiply_fusion
  508.4 3.4 copy.124
  511.8 3.4 all_to_all.85
  515.2 3.4 mul.45
  518.6 3.0 copy.106
  521.6 2.0 copy.125
  523.5 2.6 reshape.97
  526.2 1.6 copy.105
  (38 shorter events, 3.6 us)
Async XLA Ops:
  8.0 120.9 %copy-start = (f32[512,512]{1,0:T(8,128)S(1)}, f32[512,512]{1,0:T(8,128)}, u32[]{:S(2)}) copy-start(f32[512,512]{1,0:T(8,128)} %param.11) | copy-start | bytes 3145732
  11.8 52.8 %all-to-all-start.3 = ((f32[1,2,512,384]{2,1,0,3:T(2,128)}), f32[1,2,512,384]{2,1,0,3:T(2,128)S(1)}, u32[]{:S(2)}, u32[]{:S(2)}) async-start(f32[1,2,512,384]{2,1,0,3:T(2,128)} %copy.114), calls=%async_computation.3 | async-start | bytes 3145728 | tf_op jit(solution)/shard_map/all_to_all | solution.py:42
  64.6 9.7 %copy-start.14 = (f32[1,2,512,384]{2,1,0,3:T(2,128)}, f32[1,2,512,384]{2,1,0,3:T(2,128)S(1)}, u32[]{:S(2)}) copy-start(f32[1,2,512,384]{2,1,0,3:T(2,128)S(1)} %all-to-all-done.3) | copy-start | bytes 4718596
  64.6 45.4 %all-to-all-start = ((f32[1,2,512,384]{2,1,0,3:T(2,128)}), f32[1,2,512,384]{2,1,0,3:T(2,128)}, u32[]{:S(2)}, u32[]{:S(2)}) async-start(f32[1,2,512,384]{2,1,0,3:T(2,128)} %copy.113), calls=%async_computation | async-start | bytes 3145728 | tf_op jit(solution)/shard_map/all_to_all | solution.py:52
  110.0 44.6 %all-to-all-start.1 = ((f32[128,8,384]{0,1,2:T(8,128)}), f32[128,8,384]{0,1,2:T(8,128)S(1)}, u32[]{:S(2)}, u32[]{:S(2)}) async-start(f32[128,8,384]{0,1,2:T(8,128)} %copy.87), calls=%async_computation.1 | async-start | bytes 3145728 | tf_op jit(solution)/shard_map/all_to_all | solution.py:43
  128.9 4.2 copy-start.15
  133.2 1.5 copy-start.6
  133.2 2.0 copy-start.8
  135.2 5.3 copy-start.3
  137.8 2.6 copy-start.9
  140.5 1.1 copy-start.1
  154.6 54.7 %all-to-all-start.5 = ((f32[128,512,6]{0,2,1:T(8,128)}), f32[128,512,6]{0,2,1:T(8,128)}, u32[]{:S(2)}, u32[]{:S(2)}) async-start(f32[128,512,6]{0,2,1:T(8,128)} %copy.98), calls=%async_computation.5 | async-start | bytes 4194304 | tf_op jit(solution)/shard_map/all_to_all | solution.py:64
  164.3 1.2 copy-start.13
  209.4 43.4 %all-to-all-start.4 = ((f32[1,128,512,6]{2,0,3,1:T(1,128)}), f32[1,128,512,6]{2,0,3,1:T(1,128)}, u32[]{:S(2)}, u32[]{:S(2)}) async-start(f32[1,128,512,6]{2,0,3,1:T(1,128)} %copy.95), calls=%async_computation.4 | async-start | bytes 3145728 | tf_op jit(solution)/shard_map/all_to_all | solution.py:49
  216.2 288.4 %all-reduce.3.cloned.1.call-start = ((), (), s32[]{:S(2)}) async-start(), calls=%async_computation.8 | async-start | bytes 2228224 | tf_op jit(solution)/shard_map/psum | solution.py:66
  216.6 4.7 copy-start.4
  216.6 4.7 copy-start.10
  221.4 2.7 copy-start.2
  224.1 1.4 copy-start.7
  225.6 3.4 copy-start.11
  225.6 3.4 copy-start.5
  232.7 295.1 %reduce-scatter.2.cloned.1.call-start = ((), (), s32[]{:S(2)}) async-start(), calls=%async_computation.7 | async-start | bytes 1966080 | tf_op jit(solution)/shard_map/reduce_scatter | solution.py:65
  236.7 1.4 copy-start.12
  252.7 268.8 %all-to-all-start.2 = ((f32[1,128,512,6]{2,0,3,1:T(1,128)}), f32[1,128,512,6]{2,0,3,1:T(1,128)S(1)}, u32[]{:S(2)}, u32[]{:S(2)}) async-start(f32[1,128,512,6]{2,0,3,1:T(1,128)} %copy.90), calls=%async_computation.2 | async-start | bytes 3145728 | tf_op jit(solution)/shard_map/all_to_all | solution.py:63
Sparse Core Ops, SparseCore 0:
  232.8 271.7 all-reduce.2
Sparse Core Ops, SparseCore 1:
  236.8 48.6 reduce-scatter.1
where the time goes:
time: 543 us; the launch traced here: 535 us
  waiting for transfers between devices  369 us (68%)
  local copies, waits for them, and re-layouts  57.9 us (11%)
  starting transfers between devices  47 us (9%)
  matrix products  35 us (6%)
  between operations  16 us (3%)
  other arithmetic  10.5 us (2%)
    psum x1, waiting for transfers between devices, body(): lax.psum((first_grad, second_grad), ('seq', 'dp'))  242 us
    all_to_all x1, waiting for transfers between devices, body(): lax.all_to_all(kernel_cols_grad, 'seq', split_axis=1, concat_axis=2, tile...  38.3 us
    all_to_all x1, waiting for transfers between devices, body(): lax.all_to_all(grad_mixed, 'seq', split_axis=3, concat_axis=1, tiled=True)  35.7 us
    all_to_all x1, waiting for transfers between devices, body(): lax.all_to_all(source, 'seq', split_axis=3, concat_axis=1, tiled=True)  32.9 us
    unnamed x36, local copies, waits for them, and re-layouts  14.9 us
    all_to_all x1, starting transfers between devices, body(): lax.all_to_all(source, 'seq', split_axis=3, concat_axis=1, tiled=True)  13 us
  transfers between devices with their start and end apart: 8, of which 6 were waited for; matrix products, arithmetic and copies ran while one was open for 17% of the time, Pallas kernels for 0%

commit v1 on v0

--- a/solution.py
+++ b/solution.py
@@ -63,7 +63,7 @@
     grad_source = lax.all_to_all(grad_full, "seq", split_axis=1, concat_axis=3, tiled=True)
     kernel_term = lax.all_to_all(kernel_cols_grad, "seq", split_axis=1, concat_axis=2, tiled=True)
     grad_kernel = lax.psum_scatter(kernel_term, "dp", scatter_dimension=0, tiled=True)
-    first_total, second_total = lax.psum((first_grad, second_grad), ("seq", "dp"))
+    first_total, second_total = lax.psum(lax.psum((first_grad, second_grad), "seq"), "dp")
     sequences = batch * lax.axis_size("dp")
     first_scale = 1.0 / math.sqrt(sequences * block * channels)
     second_scale = 1.0 / math.sqrt(sequences * blocks * channels)

time: 543 us -> 922 us (1.70)
  waiting for transfers between devices: 369 us -> 740 us
  starting transfers between devices: 47 us -> 57.7 us
    psum x1 -> x2, waiting for transfers between devices: 242 us -> 607 us  [the longest x1 571 us: body(): lax.psum((first_grad, second_grad), 'seq')]
    reduce_scatter x1, waiting for transfers between devices: 0.01 us -> 20.5 us  [body(): lax.psum_scatter(kernel_term, 'dp', scatter_dimension=0, tiled=True)]
    all_to_all x1, starting transfers between devices: 6.81 us -> 17.9 us  [body(): lax.all_to_all(grad_full, 'seq', split_axis=1, concat_axis=3, tiled=True)]
    all_to_all x1, waiting for transfers between devices: 9.26 us -> 0.01 us  [body(): lax.all_to_all(full_mixed, 'seq', split_axis=1, concat_axis=3, tiled=True)]
  transfers between devices with their start and end apart: 8 -> 9, of which waited for: 6 -> 7; matrix products, arithmetic and copies ran while one was open for 17% -> 10% of each run, Pallas kernels for 0% -> 0%
where the time goes in v1:
time: 922 us; the launch traced here: 914 us
  waiting for transfers between devices  740 us (80%)
  local copies, waits for them, and re-layouts  57.8 us (6%)
  starting transfers between devices  57.7 us (6%)
  matrix products  34.5 us (4%)
  between operations  14.3 us (2%)
  other arithmetic  10.5 us (1%)
    psum x1, waiting for transfers between devices, body(): lax.psum((first_grad, second_grad), 'seq')  571 us
    psum x1, waiting for transfers between devices, body(): lax.psum(lax.psum((first_grad, second_grad), 'seq'), 'dp')  36.5 us
    all_to_all x1, waiting for transfers between devices, body(): lax.all_to_all(grad_mixed, 'seq', split_axis=3, concat_axis=1, tiled=True)  35.8 us
    all_to_all x1, waiting for transfers between devices, body(): lax.all_to_all(source, 'seq', split_axis=3, concat_axis=1, tiled=True)  32.9 us
    all_to_all x1, waiting for transfers between devices, body(): lax.all_to_all(kernel_cols_grad, 'seq', split_axis=1, concat_axis=2, tile...  32.3 us
    reduce_scatter x1, waiting for transfers between devices, body(): lax.psum_scatter(kernel_term, 'dp', scatter_dimension=0, tiled=True)  20.5 us
  transfers between devices with their start and end apart: 9, of which 7 were waited for; matrix products, arithmetic and copies ran while one was open for 10% of the time, Pallas kernels for 0%

profile of v1, /device:TPU:6, one launch (start us, length us, event | category | flops | bytes accessed | tf_op | source)
XLA Modules:
  0.0 914.4 jit_solution(13545571677379559737)
XLA Ops:
  7.2 3.8 copy.114
  10.9 13.0 %all-to-all-start.3 = ((f32[1,2,512,384]{2,1,0,3:T(2,128)}), f32[1,2,512,384]{2,1,0,3:T(2,128)S(1)}, u32[]{:S(2)}, u32[]{:S(2)}) async-start(f32[1,2,512,384]{2,1,0,3:T(2,128)} %copy.114), calls=%async_computation.3 | async-start | bytes 3145728 | tf_op jit(solution)/shard_map/all_to_all | solution.py:42
  24.0 3.2 mul.41
  27.1 3.7 copy.113
  30.8 32.9 %all-to-all-done.3 = f32[1,2,512,384]{2,1,0,3:T(2,128)S(1)} async-done(((f32[1,2,512,384]{2,1,0,3:T(2,128)}), f32[1,2,512,384]{2,1,0,3:T(2,128)S(1)}, u32[]{:S(2)}, u32[]{:S(2)}) %all-to-all-start.3) | async-done | bytes 1572896 | tf_op jit(solution)/shard_map/all_to_all | solution.py:42
  63.7 6.6 all-to-all-start
  70.3 3.0 copy.87
  73.4 35.8 %all-to-all-done = f32[1,2,512,384]{2,1,0,3:T(2,128)} async-done(((f32[1,2,512,384]{2,1,0,3:T(2,128)}), f32[1,2,512,384]{2,1,0,3:T(2,128)}, u32[]{:S(2)}, u32[]{:S(2)}) %all-to-all-start) | async-done | bytes 1572896 | tf_op jit(solution)/shard_map/all_to_all | solution.py:52
  109.2 6.3 all-to-all-start.1
  115.5 3.1 copy.93
  118.5 3.1 reshape.99
  121.7 3.1 copy.85
  124.8 3.3 reshape.93
  128.1 4.2 fusion.44
  132.3 1.5 fusion.10
  134.3 2.7 fusion.47
  137.0 2.6 fusion.14
  140.8 2.3 copy.98
  143.1 10.7 %all-to-all-done.1 = f32[128,8,384]{0,1,2:T(8,128)S(1)} async-done(((f32[128,8,384]{0,1,2:T(8,128)}), f32[128,8,384]{0,1,2:T(8,128)S(1)}, u32[]{:S(2)}, u32[]{:S(2)}) %all-to-all-start.1) | async-done | bytes 1572896 | tf_op jit(solution)/shard_map/all_to_all | solution.py:43
  153.8 6.9 all-to-all-start.5
  160.7 2.8 fusion.53
  164.7 2.7 fusion.19
  167.4 2.8 copy.95
  170.2 2.6 fusion.34
  172.9 3.4 fusion.40
  176.2 32.3 %all-to-all-done.5 = f32[128,512,6]{0,2,1:T(8,128)} async-done(((f32[128,512,6]{0,2,1:T(8,128)}), f32[128,512,6]{0,2,1:T(8,128)}, u32[]{:S(2)}, u32[]{:S(2)}) %all-to-all-start.5) | async-done | bytes 1572896 | tf_op jit(solution)/shard_map/all_to_all | solution.py:64
  208.5 6.8 all-to-all-start.4
  215.4 3.0 fusion.50
  218.4 2.7 fusion.25
  221.1 3.7 fusion.31
  224.9 570.8 %all-reduce.5.cloned.1.call-done = (f32[128,128]{1,0:T(8,128)}, f32[512,512]{1,0:T(8,128)}) async-done(((f32[128,128]{1,0:T(8,128)}, f32[512,512]{1,0:T(8,128)}), (f32[128,128]{1,0:T(8,128)}, f32[512,512]{1,0:T(8,128)})) %all-reduce.5.cloned.1.call-update) | async-done | bytes 1114128 | tf_op jit(solution)/shard_map/psum | solution.py:66
  795.9 1.9 copy.100
  797.8 1.8 copy.101
  801.0 2.7 fusion.22
  803.7 2.8 copy.90
  806.4 17.9 %all-to-all-start.2 = ((f32[1,128,512,6]{2,0,3,1:T(1,128)}), f32[1,128,512,6]{2,0,3,1:T(1,128)S(1)}, u32[]{:S(2)}, u32[]{:S(2)}) async-start(f32[1,128,512,6]{2,0,3,1:T(1,128)} %copy.90), calls=%async_computation.2 | async-start | bytes 3145728 | tf_op jit(solution)/shard_map/all_to_all | solution.py:63
  824.3 3.0 copy.97
  827.4 36.5 %all-reduce.7.cloned.1.call-done = (f32[128,128]{1,0:T(8,128)}, f32[512,512]{1,0:T(8,128)}) async-done(((f32[128,128]{1,0:T(8,128)}, f32[512,512]{1,0:T(8,128)}), (f32[128,128]{1,0:T(8,128)}, f32[512,512]{1,0:T(8,128)})) %all-reduce.7.cloned.1.call-update) | async-done | bytes 1114128 | tf_op jit(solution)/shard_map/psum | solution.py:66
  863.9 1.5 broadcast_multiply_fusion.1
  865.4 2.3 broadcast_multiply_fusion
  867.7 3.4 copy.124
  871.1 3.4 all_to_all.85
  874.5 3.4 mul.45
  877.9 3.0 copy.106
  881.0 2.0 copy.125
  882.9 2.6 reshape.97
  885.5 1.6 copy.105
  887.2 20.5 %reduce-scatter.2.cloned.1.call-done = f32[32,8,384]{2,1,0:T(8,128)} async-done(((f32[128,8,384]{2,1,0:T(8,128)}), f32[32,8,384]{2,1,0:T(8,128)}) %reduce-scatter.2.cloned.1.call-update) | async-done | bytes 393232 | tf_op jit(solution)/shard_map/reduce_scatter | solution.py:65
  (45 shorter events, 4.6 us)
Async XLA Ops:
  7.2 120.9 %copy-start = (f32[512,512]{1,0:T(8,128)S(1)}, f32[512,512]{1,0:T(8,128)}, u32[]{:S(2)}) copy-start(f32[512,512]{1,0:T(8,128)} %param.11) | copy-start | bytes 3145732
  10.9 52.8 %all-to-all-start.3 = ((f32[1,2,512,384]{2,1,0,3:T(2,128)}), f32[1,2,512,384]{2,1,0,3:T(2,128)S(1)}, u32[]{:S(2)}, u32[]{:S(2)}) async-start(f32[1,2,512,384]{2,1,0,3:T(2,128)} %copy.114), calls=%async_computation.3 | async-start | bytes 3145728 | tf_op jit(solution)/shard_map/all_to_all | solution.py:42
  63.7 9.6 %copy-start.16 = (f32[1,2,512,384]{2,1,0,3:T(2,128)}, f32[1,2,512,384]{2,1,0,3:T(2,128)S(1)}, u32[]{:S(2)}) copy-start(f32[1,2,512,384]{2,1,0,3:T(2,128)S(1)} %all-to-all-done.3) | copy-start | bytes 4718596
  63.7 45.4 %all-to-all-start = ((f32[1,2,512,384]{2,1,0,3:T(2,128)}), f32[1,2,512,384]{2,1,0,3:T(2,128)}, u32[]{:S(2)}, u32[]{:S(2)}) async-start(f32[1,2,512,384]{2,1,0,3:T(2,128)} %copy.113), calls=%async_computation | async-start | bytes 3145728 | tf_op jit(solution)/shard_map/all_to_all | solution.py:52
  109.2 44.6 %all-to-all-start.1 = ((f32[128,8,384]{0,1,2:T(8,128)}), f32[128,8,384]{0,1,2:T(8,128)S(1)}, u32[]{:S(2)}, u32[]{:S(2)}) async-start(f32[128,8,384]{0,1,2:T(8,128)} %copy.87), calls=%async_computation.1 | async-start | bytes 3145728 | tf_op jit(solution)/shard_map/all_to_all | solution.py:43
  128.1 4.2 copy-start.17
  132.3 1.5 copy-start.8
  132.3 2.0 copy-start.6
  134.3 5.3 copy-start.3
  137.0 2.6 copy-start.10
  139.6 1.1 copy-start.1
  153.8 54.7 %all-to-all-start.5 = ((f32[128,512,6]{0,2,1:T(8,128)}), f32[128,512,6]{0,2,1:T(8,128)}, u32[]{:S(2)}, u32[]{:S(2)}) async-start(f32[128,512,6]{0,2,1:T(8,128)} %copy.98), calls=%async_computation.5 | async-start | bytes 4194304 | tf_op jit(solution)/shard_map/all_to_all | solution.py:64
  163.5 1.2 copy-start.14
  167.4 2.8 copy-start.4
  167.4 2.8 copy-start.11
  170.2 2.7 copy-start.2
  170.2 2.7 copy-start.9
  208.5 597.9 %all-to-all-start.4 = ((f32[1,128,512,6]{2,0,3,1:T(1,128)}), f32[1,128,512,6]{2,0,3,1:T(1,128)}, u32[]{:S(2)}, u32[]{:S(2)}) async-start(f32[1,128,512,6]{2,0,3,1:T(1,128)} %copy.95), calls=%async_computation.4 | async-start | bytes 3145728 | tf_op jit(solution)/shard_map/all_to_all | solution.py:49
  215.3 580.3 %all-reduce.5.cloned.1.call-start = ((), (), s32[]{:S(2)}) async-start(), calls=%async_computation.8 | async-start | bytes 2228224 | tf_op jit(solution)/shard_map/psum | solution.py:66
  215.4 3.0 copy-start.7
  215.4 3.0 copy-start.15
  218.4 2.7 copy-start.12
  218.4 2.7 copy-start.5
  224.8 639.1 %all-reduce.7.cloned.1.call-start = ((), (), s32[]{:S(2)}) async-start(), calls=%async_computation.9 | async-start | bytes 2228224 | tf_op jit(solution)/shard_map/psum | solution.py:66
  795.7 111.9 %reduce-scatter.2.cloned.1.call-start = ((), (), s32[]{:S(2)}) async-start(), calls=%async_computation.7 | async-start | bytes 1966080 | tf_op jit(solution)/shard_map/reduce_scatter | solution.py:65
  799.6 1.4 copy-start.13
  806.4 74.5 %all-to-all-start.2 = ((f32[1,128,512,6]{2,0,3,1:T(1,128)}), f32[1,128,512,6]{2,0,3,1:T(1,128)S(1)}, u32[]{:S(2)}, u32[]{:S(2)}) async-start(f32[1,128,512,6]{2,0,3,1:T(1,128)} %copy.90), calls=%async_computation.2 | async-start | bytes 3145728 | tf_op jit(solution)/shard_map/all_to_all | solution.py:63
Sparse Core Ops, SparseCore 0:
  225.0 570.6 all-reduce.4
  798.6 65.2 all-reduce.6
  867.3 40.2 reduce-scatter.1
